TPU v7x, 32 devices: a whole 2x2x4 slice. The times are simulated.
32 devices in a mesh: groups: 2 (over x), tenant: 16 (over z, y, core).
Axes of the slice: x: 2, y: 2, z: 4, core: 2. Of those that a mesh axis runs over, the one named last changes fastest.
Arguments:
- tokens: bfloat16 [4096, 8192], P(('groups', 'tenant')), parts along dimension 0, may hold values from -6 to 6
- cotangent: bfloat16 [4096, 8192], P(('groups', 'tenant')), parts along dimension 0, may hold values from -6 to 6
- down_a: float32 [16, 64, 8192], P('tenant'), may hold values from -0.0625 to 0.0625
- up_b: float32 [16, 64, 8192], P('tenant'), may hold values from -0.0625 to 0.0625
- block_tenant: int32 [32], P('groups'), parts along dimension 0, may hold values from 0 to 15, as said below
- tenant_slot: int32 [16], replicated, may hold values from 0 to 15, each once
Outputs:
- grad_tokens: bfloat16 [4096, 8192], P(('groups', 'tenant')), parts along dimension 0
- grad_down: bfloat16 [32, 64, 8192], P(('groups', 'tenant')), parts along dimension 0
- grad_up: bfloat16 [32, 64, 8192], P(('groups', 'tenant')), parts along dimension 0
There are 2 independent parts, one for each index of `groups`. A program takes and returns all parts, laid end to end along the dimension named above; an argument that names none is the same for every part. Nothing has to cross between parts.
Inputs may be any that keep to these rules, and one draw needn't show every extreme that they name: `block_tenant`: no tenant owns more than 4 blocks, and one tenant owns exactly 4. `tenant_slot`: each tenant has its own storage row.
All inputs are finite; a program needn't handle non-finite values.
Results may differ from a plain program's by a relative error of at most 0.0064.
Values may be sent and summed in bfloat16 or wider, within the bound.
A program may use at most 128 MiB of HBM per device.

v0:
```python
import jax
import jax.numpy as jnp
from jax import lax
from jax.sharding import PartitionSpec as P

adapter_scale = 2.0


def column_plan(tokens, cotangent, down_a, up_b, slot_of_block):
    devices = lax.axis_size("tenant")
    rank_size = down_a.shape[1]
    tenants = down_a.shape[0] * devices
    blocks = slot_of_block.shape[0]
    block_rows = tokens.shape[0] * devices // blocks
    x_cols, g_cols = (
        lax.all_to_all(tokens, "tenant", split_axis=1, concat_axis=0, tiled=True),
        lax.all_to_all(cotangent, "tenant", split_axis=1, concat_axis=0, tiled=True),
    )
    columns = x_cols.shape[1]
    down_cols, up_cols = (
        lax.all_to_all(
            down_a.astype(jnp.bfloat16), "tenant", split_axis=2, concat_axis=0, tiled=True
        ),
        lax.all_to_all(
            up_b.astype(jnp.bfloat16), "tenant", split_axis=2, concat_axis=0, tiled=True
        ),
    )
    select = slot_of_block[:, None] == jnp.arange(tenants, dtype=jnp.int32)[None, :]
    table = jnp.concatenate([down_cols, up_cols], axis=1).reshape(tenants, 2 * rank_size * columns)
    picked = jnp.dot(select.astype(jnp.bfloat16), table, preferred_element_type=jnp.float32)
    picked = picked.astype(jnp.bfloat16).reshape(blocks, 2 * rank_size, columns)
    down_blk = picked[:, :rank_size]
    up_blk = picked[:, rank_size:]
    token_blocks = x_cols.reshape(blocks, block_rows, columns)
    cotan_blocks = g_cols.reshape(blocks, block_rows, columns)
    forward_part = jnp.einsum(
        "bkc,brc->bkr", token_blocks, down_blk, preferred_element_type=jnp.float32
    )
    backward_piece = adapter_scale * jnp.einsum(
        "bkc,brc->bkr", cotan_blocks, up_blk, preferred_element_type=jnp.float32
    )
    partial_sum = jnp.concatenate([forward_part, backward_piece], axis=2).reshape(
        blocks * block_rows, 2 * rank_size
    )
    ranked = lax.psum(partial_sum, "tenant").astype(jnp.bfloat16)
    ranked = ranked.reshape(blocks, block_rows, 2 * rank_size)
    forward_rank_rows = ranked[:, :, :rank_size]
    backward_rank_rows = ranked[:, :, rank_size:]
    grad_cols = jnp.einsum(
        "bkr,brc->bkc", backward_rank_rows, down_blk, preferred_element_type=jnp.float32
    )
    grad_cols = grad_cols.astype(jnp.bfloat16).reshape(blocks * block_rows, columns)
    term_down = jnp.einsum(
        "bkr,bkc->brc", backward_rank_rows, token_blocks, preferred_element_type=jnp.float32
    )
    up_term_value = adapter_scale * jnp.einsum(
        "bkr,bkc->brc", forward_rank_rows, cotan_blocks, preferred_element_type=jnp.float32
    )
    grads_both = jnp.concatenate([term_down, up_term_value], axis=1).reshape(
        blocks, 2 * rank_size * columns
    )
    per_tenant = jnp.einsum(
        "bt,bx->tx", select.astype(jnp.float32), grads_both, precision=lax.Precision.HIGHEST
    )
    per_tenant = per_tenant.reshape(tenants, 2 * rank_size, columns).astype(jnp.bfloat16)
    grad_down, grad_up = (
        lax.all_to_all(
            per_tenant[:, :rank_size], "tenant", split_axis=0, concat_axis=2, tiled=True
        ),
        lax.all_to_all(
            per_tenant[:, rank_size:], "tenant", split_axis=0, concat_axis=2, tiled=True
        ),
    )
    grad_tokens = lax.all_to_all(grad_cols, "tenant", split_axis=0, concat_axis=1, tiled=True)
    return (grad_tokens, grad_down, grad_up)


def shards(tokens, cotangent, down_a, up_b, block_tenant, tenant_slot):
    slot_of_block = tenant_slot[block_tenant]
    return column_plan(tokens, cotangent, down_a, up_b, slot_of_block)


def solution(mesh):
    return jax.shard_map(
        shards,
        mesh=mesh,
        in_specs=(
            P(("groups", "tenant"), None),
            P(("groups", "tenant"), None),
            P("tenant", None, None),
            P("tenant", None, None),
            P("groups"),
            P(),
        ),
        out_specs=(
            P(("groups", "tenant"), None),
            P(("groups", "tenant"), None, None),
            P(("groups", "tenant"), None, None),
        ),
        check_vma=False,
    )
```

profile of v0, /device:TPU:2, one launch (start us, length us, event | category | flops | bytes accessed | tf_op | source)
XLA Modules:
  0.0 455.0 jit_solution(12365542430147940811)
XLA Ops:
  0.6 1.7 convert_element_type.21
  2.4 6.8 %copy.39 = bf16[1,64,8192]{1,0,2:T(2,128)(2,1)} copy(bf16[1,64,8192]{2,1,0:T(8,128)(2,1)S(1)} %convert_element_type.21) | data formatting | bytes 2097152 | tf_op jit(solution)/shard_map/convert_element_type | solution.py:25
  9.6 45.2 %reduce = bf16[8192,64]{1,0:T(8,128)(2,1)S(1)} reduce(bf16[8192,1,64]{2,1,0:T(2,128)(2,1)} %bitcast.83, bf16[]{:T(256)} %broadcast.17), dimensions={1}, to_apply=%bitcast.74.reduce_sub_computation | reduce | bytes 2097154
  54.9 2.3 reshape.54
  57.2 5.9 %all-to-all-start.1 = ((bf16[16,2,16384]{2,1,0:T(2,128)(2,1)}), bf16[16,2,16384]{2,1,0:T(2,128)(2,1)S(1)}, u32[]{:S(2)}, u32[]{:S(2)}) async-start(bf16[16,2,16384]{2,1,0:T(2,128)(2,1)} %reshape.54), calls=%async_computation.1 | async-start | bytes 2097152 | tf_op jit(solution)/shard_map/all_to_all | solution.py:24
  63.1 1.7 convert_element_type.20
  64.8 6.8 %copy.37 = bf16[1,64,8192]{1,0,2:T(2,128)(2,1)} copy(bf16[1,64,8192]{2,1,0:T(8,128)(2,1)S(1)} %convert_element_type.20) | data formatting | bytes 2097152 | tf_op jit(solution)/shard_map/convert_element_type | solution.py:22
  71.6 45.2 %reduce.1 = bf16[8192,64]{1,0:T(8,128)(2,1)S(1)} reduce(bf16[8192,1,64]{2,1,0:T(2,128)(2,1)} %bitcast.84, bf16[]{:T(256)} %broadcast.17), dimensions={1}, to_apply=%bitcast.76.reduce_sub_computation | reduce | bytes 2097154
  116.8 2.3 reshape.56
  119.1 6.1 %all-to-all-start = ((bf16[16,2,16384]{2,1,0:T(2,128)(2,1)}), bf16[16,2,16384]{2,1,0:T(2,128)(2,1)}, u32[]{:S(2)}, u32[]{:S(2)}) async-start(bf16[16,2,16384]{2,1,0:T(2,128)(2,1)} %reshape.56), calls=%async_computation | async-start | bytes 2097152 | tf_op jit(solution)/shard_map/all_to_all | solution.py:21
  125.2 3.2 copy.44
  128.4 2.6 copy.45
  131.0 17.2 %all-to-all-done = bf16[16,2,16384]{2,1,0:T(2,128)(2,1)} async-done(((bf16[16,2,16384]{2,1,0:T(2,128)(2,1)}), bf16[16,2,16384]{2,1,0:T(2,128)(2,1)}, u32[]{:S(2)}, u32[]{:S(2)}) %all-to-all-start) | async-done | bytes 1048608 | tf_op jit(solution)/shard_map/all_to_all | solution.py:21
  148.2 6.9 %all-to-all-start.3 = ((bf16[128,16,512]{2,0,1:T(8,128)(2,1)}), bf16[128,16,512]{2,0,1:T(8,128)(2,1)S(1)}, u32[]{:S(2)}, u32[]{:S(2)}) async-start(bf16[128,16,512]{2,0,1:T(8,128)(2,1)} %copy.45), calls=%async_computation.3 | async-start | bytes 4194304 | tf_op jit(solution)/shard_map/all_to_all | solution.py:17
  155.0 4.1 copy.42
  159.1 3.9 copy.43
  163.0 33.1 %all-to-all-done.3 = bf16[128,16,512]{2,0,1:T(8,128)(2,1)S(1)} async-done(((bf16[128,16,512]{2,0,1:T(8,128)(2,1)}), bf16[128,16,512]{2,0,1:T(8,128)(2,1)S(1)}, u32[]{:S(2)}, u32[]{:S(2)}) %all-to-all-start.3) | async-done | bytes 2097184 | tf_op jit(solution)/shard_map/all_to_all | solution.py:17
  196.1 11.3 %all-to-all-start.2 = ((bf16[128,16,512]{2,0,1:T(8,128)(2,1)}), bf16[128,16,512]{2,0,1:T(8,128)(2,1)}, u32[]{:S(2)}, u32[]{:S(2)}) async-start(bf16[128,16,512]{2,0,1:T(8,128)(2,1)} %copy.43), calls=%async_computation.2 | async-start | bytes 4194304 | tf_op jit(solution)/shard_map/all_to_all | solution.py:16
  207.5 0.7 gather_fusion
  208.1 7.0 %reshape.55 = bf16[8192,1,64]{2,1,0:T(2,128)(2,1)} reshape(bf16[16,2,16384]{2,1,0:T(2,128)(2,1)S(1)} %all-to-all-done.1) | data formatting | bytes 2097152
  215.2 8.2 %copy.40 = bf16[1,64,8192]{2,1,0:T(8,128)(2,1)S(1)} copy(bf16[1,64,8192]{1,0,2:T(2,128)(2,1)} %bitcast.85) | data formatting | bytes 2097152 | tf_op jit(solution)/shard_map/all_to_all | solution.py:24
  223.3 1.3 copy.63
  224.7 10.2 %reshape.57 = bf16[8192,1,64]{2,1,0:T(2,128)(2,1)} reshape(bf16[16,2,16384]{2,1,0:T(2,128)(2,1)} %all-to-all-done) | data formatting | bytes 2097152
  234.8 8.2 %copy.38 = bf16[1,64,8192]{2,1,0:T(8,128)(2,1)S(1)} copy(bf16[1,64,8192]{1,0,2:T(2,128)(2,1)} %bitcast.86) | data formatting | bytes 2097152 | tf_op jit(solution)/shard_map/all_to_all | solution.py:21
  243.4 0.9 copy-done.4
  244.8 0.8 convolution_convert_fusion
  245.5 0.7 copy.64
  246.2 1.3 copy-done.2
  247.5 1.6 fusion.20
  249.2 2.8 fusion.23
  252.1 1.3 copy.46
  253.4 79.1 %all-reduce.1 = bf16[2048,128]{1,0:T(8,128)(2,1)S(1)} all-reduce(f32[2048,128]{1,0:T(8,128)} %bitcast.102), channel_id=1, replica_groups=mesh['groups'=2,'tenant'=16] {'tenant'}, use_global_device_ids=true, to_apply=%region_0.0 | all-reduce | flops 262144 | bytes 1572864 | tf_op jit(solution)/shard_map/psum | solution.py:45
  333.0 2.4 fusion.7
  335.9 4.5 fusion.11
  340.4 1.1 fusion.36
  341.6 1.5 copy.51
  343.1 4.6 %all-to-all-start.5 = ((bf16[16,64,512]{2,1,0:T(8,128)(2,1)}), bf16[16,64,512]{2,1,0:T(8,128)(2,1)}, u32[]{:S(2)}, u32[]{:S(2)}) async-start(bf16[16,64,512]{2,1,0:T(8,128)(2,1)} %copy.51), calls=%async_computation.5 | async-start | bytes 2097152 | tf_op jit(solution)/shard_map/all_to_all | solution.py:67
  347.8 2.9 copy.53
  350.7 20.0 %all-to-all-done.5 = bf16[16,64,512]{2,1,0:T(8,128)(2,1)} async-done(((bf16[16,64,512]{2,1,0:T(8,128)(2,1)}), bf16[16,64,512]{2,1,0:T(8,128)(2,1)}, u32[]{:S(2)}, u32[]{:S(2)}) %all-to-all-start.5) | async-done | bytes 1048608 | tf_op jit(solution)/shard_map/all_to_all | solution.py:67
  370.7 6.9 %all-to-all-start.6 = ((bf16[16,64,512]{2,1,0:T(8,128)(2,1)}), bf16[16,64,512]{2,1,0:T(8,128)(2,1)}, u32[]{:S(2)}, u32[]{:S(2)}) async-start(bf16[16,64,512]{2,1,0:T(8,128)(2,1)} %copy.53), calls=%async_computation.6 | async-start | bytes 2097152 | tf_op jit(solution)/shard_map/all_to_all | solution.py:70
  377.6 2.1 convolution_convert_fusion.1
  379.6 20.9 %all-to-all-done.6 = bf16[16,64,512]{2,1,0:T(8,128)(2,1)} async-done(((bf16[16,64,512]{2,1,0:T(8,128)(2,1)}), bf16[16,64,512]{2,1,0:T(8,128)(2,1)}, u32[]{:S(2)}, u32[]{:S(2)}) %all-to-all-start.6) | async-done | bytes 1048608 | tf_op jit(solution)/shard_map/all_to_all | solution.py:70
  400.6 6.9 %all-to-all-start.4 = ((bf16[16,128,512]{2,1,0:T(8,128)(2,1)}), bf16[16,128,512]{2,1,0:T(8,128)(2,1)S(1)}, u32[]{:S(2)}, u32[]{:S(2)}) async-start(bf16[16,128,512]{2,1,0:T(8,128)(2,1)} %convolution_convert_fusion.1), calls=%async_computation.4 | async-start | bytes 4194304 | tf_op jit(solution)/shard_map/all_to_all | solution.py:74
  407.4 2.3 copy.60
  409.7 2.3 copy.61
  412.0 36.5 %all-to-all-done.4 = bf16[16,128,512]{2,1,0:T(8,128)(2,1)S(1)} async-done(((bf16[16,128,512]{2,1,0:T(8,128)(2,1)}), bf16[16,128,512]{2,1,0:T(8,128)(2,1)S(1)}, u32[]{:S(2)}, u32[]{:S(2)}) %all-to-all-start.4) | async-done | bytes 2097184 | tf_op jit(solution)/shard_map/all_to_all | solution.py:74
  448.5 2.4 copy.48
  450.9 4.1 copy.55
  (24 shorter events, 2.6 us)
Async XLA Ops:
  0.6 206.8 %copy-start = (s32[16]{0:T(128)S(1)}, s32[16]{0:T(128)}, u32[]{:S(2)}) copy-start(s32[16]{0:T(128)} %param.11) | copy-start | bytes 196
  57.2 62.0 %all-to-all-start.1 = ((bf16[16,2,16384]{2,1,0:T(2,128)(2,1)}), bf16[16,2,16384]{2,1,0:T(2,128)(2,1)S(1)}, u32[]{:S(2)}, u32[]{:S(2)}) async-start(bf16[16,2,16384]{2,1,0:T(2,128)(2,1)} %reshape.54), calls=%async_computation.1 | async-start | bytes 2097152 | tf_op jit(solution)/shard_map/all_to_all | solution.py:24
  119.1 29.1 %all-to-all-start = ((bf16[16,2,16384]{2,1,0:T(2,128)(2,1)}), bf16[16,2,16384]{2,1,0:T(2,128)(2,1)}, u32[]{:S(2)}, u32[]{:S(2)}) async-start(bf16[16,2,16384]{2,1,0:T(2,128)(2,1)} %reshape.56), calls=%async_computation | async-start | bytes 2097152 | tf_op jit(solution)/shard_map/all_to_all | solution.py:21
  148.2 48.0 %all-to-all-start.3 = ((bf16[128,16,512]{2,0,1:T(8,128)(2,1)}), bf16[128,16,512]{2,0,1:T(8,128)(2,1)S(1)}, u32[]{:S(2)}, u32[]{:S(2)}) async-start(bf16[128,16,512]{2,0,1:T(8,128)(2,1)} %copy.45), calls=%async_computation.3 | async-start | bytes 4194304 | tf_op jit(solution)/shard_map/all_to_all | solution.py:17
  163.0 44.4 %copy-start.6 = (s32[16]{0:T(128)S(1)}, s32[16]{0:T(128)}, u32[]{:S(2)}) copy-start(s32[16]{0:T(128)} %param.10) | copy-start | bytes 196
  196.1 53.0 %all-to-all-start.2 = ((bf16[128,16,512]{2,0,1:T(8,128)(2,1)}), bf16[128,16,512]{2,0,1:T(8,128)(2,1)}, u32[]{:S(2)}, u32[]{:S(2)}) async-start(bf16[128,16,512]{2,0,1:T(8,128)(2,1)} %copy.43), calls=%async_computation.2 | async-start | bytes 4194304 | tf_op jit(solution)/shard_map/all_to_all | solution.py:16
  243.0 1.2 copy-start.4
  246.2 1.3 copy-start.2
  249.2 2.8 copy-start.5
  343.1 27.5 %all-to-all-start.5 = ((bf16[16,64,512]{2,1,0:T(8,128)(2,1)}), bf16[16,64,512]{2,1,0:T(8,128)(2,1)}, u32[]{:S(2)}, u32[]{:S(2)}) async-start(bf16[16,64,512]{2,1,0:T(8,128)(2,1)} %copy.51), calls=%async_computation.5 | async-start | bytes 2097152 | tf_op jit(solution)/shard_map/all_to_all | solution.py:67
  347.7 29.8 %copy-start.3 = (bf16[2,8,128,512]{3,2,1,0:T(8,128)(2,1)S(1)}, bf16[2,8,128,512]{3,2,1,0:T(8,128)(2,1)}, u32[]{:S(2)}) copy-start(bf16[2,8,128,512]{3,2,1,0:T(8,128)(2,1)} %copy-done.2) | copy-start | bytes 6291460
  370.7 29.9 %all-to-all-start.6 = ((bf16[16,64,512]{2,1,0:T(8,128)(2,1)}), bf16[16,64,512]{2,1,0:T(8,128)(2,1)}, u32[]{:S(2)}, u32[]{:S(2)}) async-start(bf16[16,64,512]{2,1,0:T(8,128)(2,1)} %copy.53), calls=%async_computation.6 | async-start | bytes 2097152 | tf_op jit(solution)/shard_map/all_to_all | solution.py:70
  400.6 48.0 %all-to-all-start.4 = ((bf16[16,128,512]{2,1,0:T(8,128)(2,1)}), bf16[16,128,512]{2,1,0:T(8,128)(2,1)S(1)}, u32[]{:S(2)}, u32[]{:S(2)}) async-start(bf16[16,128,512]{2,1,0:T(8,128)(2,1)} %convolution_convert_fusion.1), calls=%async_computation.4 | async-start | bytes 4194304 | tf_op jit(solution)/shard_map/all_to_all | solution.py:74
  450.9 4.1 copy-start.1
where the time goes:
time: 464 us; the launch traced here: 455 us
  waiting for transfers between devices  128 us (28%)
  other arithmetic  94.7 us (20%)
  local copies, waits for them, and re-layouts  89.6 us (19%)
  blocking collectives  79.1 us (17%)
  starting transfers between devices  48.5 us (10%)
  matrix products  14.6 us (3%)
    unnamed x3, other arithmetic  90.6 us
    psum x1, blocking collectives, column_plan(): ranked = lax.psum(partial_sum, 'tenant').astype(jnp.bfloat16)  79.1 us
    unnamed x25, local copies, waits for them, and re-layouts  38.3 us
    all_to_all x1, waiting for transfers between devices, column_plan(): lax.all_to_all(grad_cols, 'tenant', split_axis=0, concat_axis=1, tiled=True)  36.5 us
    all_to_all x1, waiting for transfers between devices, column_plan(): lax.all_to_all(cotangent, 'tenant', split_axis=1, concat_axis=0, tiled=True)  33.1 us
    all_to_all x1, waiting for transfers between devices, column_plan(): lax.all_to_all(per_tenant[:, rank_size:], 'tenant', split_axis=0, concat_...  20.9 us
    all_to_all x1, waiting for transfers between devices, column_plan(): lax.all_to_all(per_tenant[:, :rank_size], 'tenant', split_axis=0, concat_...  20 us
    all_to_all x1, waiting for transfers between devices, column_plan(): lax.all_to_all(down_a.astype(jnp.bfloat16), 'tenant', split_axis=2, conca...  17.2 us
  transfers between devices with their start and end apart: 7, of which 5 were waited for; matrix products, arithmetic and copies ran while one was open for 26% of the time, Pallas kernels for 0%

commit v1 on v0

v1 whole, which is shorter than its diff:
```python
import functools

import jax
import jax.numpy as jnp
from jax import lax
from jax.experimental import pallas as pl
from jax.experimental.pallas import tpu as pltpu
from jax.sharding import PartitionSpec as P

adapter_scale = 2.0
MOST = 4
MESH = pl.DeviceIdType.MESH


def wait_bytes(ref, sem):
    pltpu.make_async_copy(ref, ref, sem).wait()


def kernel(
    groups, n,
    tok_h, cot_h, down_h, up_h, bt_v, ts_s,
    gt_h, gd_h, gu_h,
    raw, low, recv1_u, recv1_d, stage2, recv2, stage3, recv3_u, recv3_d, stage4, tok_v, cot_v, gt_v, bt_all, bt_s,
    in_sem, bt_send, bt_recv, send_sem, recv_sem, gt_sem,
):
    recv1, recv3 = (recv1_u, recv1_d), (recv3_u, recv3_d)
    width = tok_h.shape[1]
    w = width // n
    ng = n // groups
    g = lax.axis_index("groups")
    me = lax.axis_index("tenant")
    side = me // ng
    r_me = me % ng
    c_me = g * ng + r_me

    def cols(c):
        return pl.ds(pl.multiple_of(c * w, w), w)

    share = pl.ds(pl.multiple_of(g * (ng * w), ng * w), ng * w)
    loads = [
        pltpu.make_async_copy(up_h.at[0, :, share], raw.at[0], in_sem.at[0]),
        pltpu.make_async_copy(down_h.at[0, :, share], raw.at[1], in_sem.at[1]),
        pltpu.make_async_copy(cot_h, cot_v, in_sem.at[2]),
        pltpu.make_async_copy(tok_h, tok_v, in_sem.at[3]),
    ]
    for load in loads:
        load.start()

    barrier = pltpu.get_barrier_semaphore()

    @pl.loop(1, n)
    def _(k):
        pl.semaphore_signal(barrier, inc=1, device_id=(g, (me + k) % n), device_id_type=MESH)

    for dg in range(1, groups):
        @pl.loop(0, ng)
        def _(r):
            pl.semaphore_signal(
                barrier, inc=1, device_id=((g + dg) % groups, side * ng + r), device_id_type=MESH
            )

    def cast(q):
        loads[q].wait()

        @pl.loop(0, ng)
        def _(r):
            low[q, r] = raw[q, :, cols(r)].astype(jnp.bfloat16)

    cast(0)
    for q in range(2):
        recv3[q][n] = jnp.zeros(recv3[q].shape[1:], jnp.bfloat16)
    pl.semaphore_wait(barrier, n - 1 + (groups - 1) * ng)

    own_map = pltpu.make_async_copy(bt_v, bt_all.at[g], bt_recv)
    own_map.start()
    for dg in range(1, groups):
        pltpu.make_async_remote_copy(
            src_ref=bt_v, dst_ref=bt_all.at[g], send_sem=bt_send.at[dg], recv_sem=bt_recv,
            device_id=((g + dg) % groups, me), device_id_type=MESH,
        ).start()

    def send(here, src, dst, hop, q, device):
        @pl.when(here)
        def _():
            pltpu.make_async_copy(src, dst, recv_sem.at[hop, q]).start()

        @pl.when(jnp.logical_not(here))
        def _():
            pltpu.make_async_remote_copy(
                src_ref=src, dst_ref=dst, send_sem=send_sem.at[hop, q], recv_sem=recv_sem.at[hop, q],
                device_id=device, device_id_type=MESH,
            ).start()

    def hop1(q):
        @pl.loop(0, n)
        def _(k):
            to = (me + n - 1 - k) % n
            send(to == me, low.at[q, to % ng], recv1[q].at[me], 0, q, (g, to))

    hop1(0)
    cast(1)
    hop1(1)

    wait_bytes(bt_all, bt_recv)
    to_scalar = pltpu.make_async_copy(bt_all, bt_s, in_sem.at[4])
    to_scalar.start()
    to_scalar.wait()

    def hop2(q):
        wait_bytes(recv1[q], recv_sem.at[0, q])
        for dg in range(groups):
            to_g = (g + dg) % groups

            @pl.loop(0, ng)
            def _(k):
                to = side * ng + (r_me + k) % ng
                slot = ts_s[bt_s[to_g, 0, to]]
                at = dg * ng + k
                stage2[q, at] = recv1[q][slot]
                here = (k == 0) if dg == 0 else (k < 0)
                send(here, stage2.at[q, at], recv2.at[q, c_me], 1, q, (to_g, to))

    hop2(0)
    hop2(1)

    block_rows = tok_h.shape[0]
    rank = down_h.shape[1]

    def rank_rows(rows_v, q):
        def step(c, total):
            return total + lax.dot_general(
                rows_v[:, cols(c)], recv2[q, c], (((1,), (1,)), ((), ())),
                preferred_element_type=jnp.float32,
            )
        return lax.fori_loop(0, n, step, jnp.zeros((block_rows, rank), jnp.float32))

    def hop3(q, left, rows_v, scale):
        @pl.loop(0, n)
        def _(k):
            to = (me + n - 1 - k) % n
            term = scale * jnp.dot(left, rows_v[:, cols(to)], preferred_element_type=jnp.float32)
            stage3[q, to] = term.astype(jnp.bfloat16)
            send(to == me, stage3.at[q, to], recv3[q].at[me], 2, q, (g, to))

    wait_bytes(recv2.at[0], recv_sem.at[1, 0])
    loads[2].wait()
    loads[3].wait()
    backward = adapter_scale * rank_rows(cot_v, 0)
    hop3(0, backward.T.astype(jnp.bfloat16), tok_v, 1.0)
    backward = backward.astype(jnp.bfloat16)

    wait_bytes(recv2.at[1], recv_sem.at[1, 1])
    forward = rank_rows(tok_v, 1)
    hop3(1, forward.T.astype(jnp.bfloat16), cot_v, adapter_scale)

    @pl.loop(0, n)
    def _(c):
        gt_v[:, cols(c)] = jnp.dot(
            backward, recv2[1, c], preferred_element_type=jnp.float32
        ).astype(jnp.bfloat16)

    gt_out = pltpu.make_async_copy(gt_v, gt_h, gt_sem)
    gt_out.start()

    def hop4(q, out_h):
        wait_bytes(recv3[q].at[pl.ds(0, n)], recv_sem.at[2, q])

        @pl.loop(0, n)
        def _(k):
            to = (me + n - 1 - k) % n

            def find(b, found):
                hit = ts_s[bt_s[g, 0, b]] == to
                later = (b,) + found[:-1]
                return tuple(jnp.where(hit, new, old) for new, old in zip(later, found))

            found = lax.fori_loop(0, n, find, (jnp.int32(n),) * MOST)
            total = recv3[q][found[0]].astype(jnp.float32)
            for b in found[1:]:
                total += recv3[q][b].astype(jnp.float32)
            stage4[q, to] = total.astype(jnp.bfloat16)
            send(to == me, stage4.at[q, to], out_h.at[0, :, cols(me)], 3, q, (g, to))

    hop4(0, gd_h)
    hop4(1, gu_h)

    wait_bytes(gd_h, recv_sem.at[3, 0])
    wait_bytes(gu_h, recv_sem.at[3, 1])
    for hop, source in enumerate((stage2, stage2, stage3, stage4)):
        for q in range(2):
            wait_bytes(source.at[q, pl.ds(0, n - 1)], send_sem.at[hop, q])
    for dg in range(1, groups):
        wait_bytes(bt_v, bt_send.at[dg])
    gt_out.wait()


def shards(groups, n, tokens, cotangent, down_a, up_b, block_tenant, tenant_slot):
    block_rows, width = tokens.shape
    rank = down_a.shape[1]
    w = width // n
    ng = n // groups
    assert down_a.shape[0] == 1 and block_tenant.shape[0] == n
    bt = jnp.zeros((8, 128), jnp.int32).at[0, :n].set(block_tenant)
    low = jnp.bfloat16
    whole = pl.BlockSpec(memory_space=pl.ANY)
    return pl.pallas_call(
        functools.partial(kernel, groups, n),
        out_shape=(
            jax.ShapeDtypeStruct((block_rows, width), low),
            jax.ShapeDtypeStruct((1, rank, width), low),
            jax.ShapeDtypeStruct((1, rank, width), low),
        ),
        in_specs=[whole] * 4 + [
            pl.BlockSpec(memory_space=pltpu.VMEM),
            pl.BlockSpec(memory_space=pltpu.SMEM),
        ],
        out_specs=(whole,) * 3,
        scratch_shapes=[
            pltpu.VMEM((2, rank, ng * w), jnp.float32),
            pltpu.VMEM((2, ng, rank, w), low),
            pltpu.VMEM((n, rank, w), low),
            pltpu.VMEM((n, rank, w), low),
            pltpu.VMEM((2, n, rank, w), low),
            pltpu.VMEM((2, n, rank, w), low),
            pltpu.VMEM((2, n, rank, w), low),
            pltpu.VMEM((n + 1, rank, w), low),
            pltpu.VMEM((n + 1, rank, w), low),
            pltpu.VMEM((2, n, rank, w), low),
            pltpu.VMEM((block_rows, width), low),
            pltpu.VMEM((block_rows, width), low),
            pltpu.VMEM((block_rows, width), low),
            pltpu.VMEM((groups, 8, 128), jnp.int32),
            pltpu.SMEM((groups, 8, 128), jnp.int32),
            pltpu.SemaphoreType.DMA((5,)),
            pltpu.SemaphoreType.DMA((groups,)),
            pltpu.SemaphoreType.DMA,
            pltpu.SemaphoreType.DMA((4, 2)),
            pltpu.SemaphoreType.DMA((4, 2)),
            pltpu.SemaphoreType.DMA,
        ],
        compiler_params=pltpu.CompilerParams(
            collective_id=0, has_side_effects=True, vmem_limit_bytes=40 * 2**20
        ),
    )(tokens, cotangent, down_a, up_b, bt, tenant_slot)


def solution(mesh):
    groups, n = mesh.shape["groups"], mesh.shape["tenant"]
    return jax.shard_map(
        functools.partial(shards, groups, n),
        mesh=mesh,
        in_specs=(
            P(("groups", "tenant"), None),
            P(("groups", "tenant"), None),
            P("tenant", None, None),
            P("tenant", None, None),
            P("groups"),
            P(),
        ),
        out_specs=(
            P(("groups", "tenant"), None),
            P(("groups", "tenant"), None, None),
            P(("groups", "tenant"), None, None),
        ),
        check_vma=False,
    )
```

time: 464 us -> 166 us (0.36); the launches traced: 455 us -> 165 us
  Pallas kernels: 0 us -> 154 us
  waiting for transfers between devices: 128 us -> 0 us
  other arithmetic: 94.7 us -> 0 us
  blocking collectives: 79.1 us -> 0 us
  local copies, waits for them, and re-layouts: 89.6 us -> 10.9 us
  starting transfers between devices: 48.5 us -> 0 us
  matrix products: 14.6 us -> 0 us
    pallas_call x0 -> x1, Pallas kernels: none -> 154 us  [shards(): pl.pallas_call(functools.partial(kernel, groups, n), out_shape=(jax.Shape...]
    all_to_all x7 -> x0, waiting for transfers between devices: 128 us -> none  [the longest x1 36.5 us: column_plan(): lax.all_to_all(grad_cols, 'tenant', split_axis=0, concat_axis=1, tiled=True)]
    unnamed x3 -> x0, other arithmetic: 90.6 us -> none
    psum x1 -> x0, blocking collectives: 79.1 us -> none  [column_plan(): ranked = lax.psum(partial_sum, 'tenant').astype(jnp.bfloat16)]
    all_to_all x7 -> x0, starting transfers between devices: 48.5 us -> none  [the longest x1 11.3 us: column_plan(): lax.all_to_all(tokens, 'tenant', split_axis=1, concat_axis=0, tiled=True)]
    all_to_all x8 -> x0, local copies, waits for them, and re-layouts: 30 us -> none  [the longest x2 8.33 us: column_plan(): lax.all_to_all(up_b.astype(jnp.bfloat16), 'tenant', split_axis=2, concat_...]
    unnamed x25 -> x13, local copies, waits for them, and re-layouts: 38.3 us -> 10.3 us
    dot_general x7 -> x0, matrix products: 14.6 us -> none  [the longest x1 4.49 us: column_plan(): jnp.einsum('bt,bx->tx', select.astype(jnp.float32), grads_both, precision...]
  transfers between devices with their start and end apart: 7 -> 0, of which waited for: 5 -> 0; matrix products, arithmetic and copies ran while one was open for 26% -> 0% of each run, Pallas kernels for 0% -> 0%
where the time goes in v1:
time: 166 us; the launch traced here: 165 us
  Pallas kernels  154 us (93%)
  local copies, waits for them, and re-layouts  10.9 us (7%)
    pallas_call x1, Pallas kernels, shards(): pl.pallas_call(functools.partial(kernel, groups, n), out_shape=(jax.Shape...  154 us
    unnamed x13, local copies, waits for them, and re-layouts  10.3 us

profile of v1, /device:TPU:2, one launch (start us, length us, event | category | flops | bytes accessed | tf_op | source)
XLA Modules:
  0.0 165.5 jit_solution(6800655276170644254)
XLA Ops:
  0.6 0.7 scatter.4.bt_v
  1.3 0.0 copy-start
  1.3 1.6 copy-done
  2.9 0.0 copy-start.1
  2.9 1.6 copy-done.1
  4.5 0.0 copy-start.2
  4.5 1.6 copy-done.2
  6.1 0.0 copy-start.3
  6.1 1.6 copy-done.3
  7.7 0.0 copy-start.4
  7.7 0.7 copy-done.4
  8.3 153.9 %shard_map.85 = (bf16[128,8192]{1,0:T(8,128)(2,1)S(1)}, bf16[1,64,8192]{2,1,0:T(8,128)(2,1)S(1)}, bf16[1,64,8192]{2,1,0:T(8,128)(2,1)S(1)}) custom-call(bf16[128,8192]{1,0:T(8,128)(2,1)S(1)} %copy-done, bf16[128,8192]{1,0:T(8,128)(2,1)S(1)} %copy-done.1, f32[1,64,8192]{2,1,0:T(8,128)S(1)} %copy-done.2, f32[1,64,8192]{2,1,0:T(8,128)S(1)} %copy-done.3, ...), custom_call_target="tpu_custom_call" | custom-call | tf_op jit(solution)/shard_map/pallas_call | solution.py:206
  162.2 1.3 copy.12
  163.5 1.0 copy.13
  164.5 1.0 copy.14
Async XLA Ops:
  1.3 1.6 copy-start
  2.9 1.6 copy-start.1
  4.5 1.6 copy-start.2
  6.1 1.6 copy-start.3
  7.7 0.7 copy-start.4
